TPU v7x, 32 devices: a whole 2x2x4 slice. The times are simulated.
32 devices in a mesh: tr: 4 (over x, core), gz: 8 (over z, y).
Axes of the slice: x: 2, y: 2, z: 4, core: 2. Of those that a mesh axis runs over, the one named last changes fastest.
Arguments:
- tokens: bfloat16 [40, 32, 8, 768], P('gz', None, 'tr'), may hold values from -6 to 6
- cotangent: bfloat16 [40, 32, 8, 768], P('gz', None, 'tr'), may hold values from -6 to 6
- gain_x: float32 [768], replicated, may hold values from 0.1 to 1.9
- wqkv_x: bfloat16 [768, 2304], P('tr'), as said below
- wo_x: bfloat16 [768, 768], P('tr'), may hold values from -0.21875 to 0.21875
- gain_z: float32 [768], replicated, may hold values from 0.1 to 1.9
- wqkv_z: bfloat16 [768, 2304], P('tr'), as said below
- wo_z: bfloat16 [768, 768], P('tr'), may hold values from -0.21875 to 0.21875
Outputs:
- grad_tokens: bfloat16 [40, 32, 8, 768], P('gz', None, 'tr')
Inputs may be any that keep to these rules, and one draw needn't show every extreme that they name: `wqkv_x`: query, key and value columns side by side, each block split into 6 heads of 128. `wqkv_z`: query, key and value columns side by side, each block split into 6 heads of 128.
All inputs are finite; a program needn't handle non-finite values.
Results may differ from a plain program's by a relative error of at most 0.038.
The roundings to bfloat16 on the way count: a program that leaves them out, or rounds other values in their place, can miss the bound.
Values may be sent and summed in bfloat16 or wider, within the bound.
A program may use at most 64 MiB of HBM per device.

v0:
```python
import math
import jax
import jax.numpy as jnp
from jax import lax
from jax.sharding import PartitionSpec as P

H = 6


def head_split(packed, index, model_width):
    piece = packed[..., index * model_width : (index + 1) * model_width]
    return piece.reshape(piece.shape[:-1] + (H, model_width // H))


def merge_heads(value):
    return value.reshape(value.shape[:-2] + (value.shape[-2] * value.shape[-1],))


def recompute(tokens_in, gain_vec, w_in, layout):
    model_width = w_in.shape[0]
    factor = 1.0 / math.sqrt(model_width // H)
    widened = tokens_in.astype(jnp.float32)
    inv_rms = lax.rsqrt(jnp.mean(widened * widened, axis=-1, keepdims=True) + 1e-06)
    normed = (widened * inv_rms * gain_vec).astype(jnp.bfloat16)
    packed = jnp.dot(normed, w_in, preferred_element_type=jnp.float32).astype(jnp.bfloat16)
    queries = head_split(packed, 0, model_width)
    key_part = head_split(packed, 1, model_width)
    values = head_split(packed, 2, model_width)
    key_form = layout.replace("l", "m")
    scores = (
        jnp.einsum(
            layout + "," + key_form + "->bhlm",
            queries,
            key_part,
            preferred_element_type=jnp.float32,
        )
        * factor
    )
    highest = jnp.max(scores, axis=-1, keepdims=True)
    expanded = jnp.exp(scores - highest)
    probs = expanded / jnp.sum(expanded, axis=-1, keepdims=True)
    return (widened, inv_rms, queries, key_part, values, probs, probs.astype(jnp.bfloat16), factor)


def forward_out(tokens_in, gain_vec, w_in, w_out, layout):
    widened, inv_rms, queries, key_part, values, probs, probs_b, factor = recompute(
        tokens_in, gain_vec, w_in, layout
    )
    key_form = layout.replace("l", "m")
    mixed = jnp.einsum(
        "bhlm," + key_form + "->" + layout, probs_b, values, preferred_element_type=jnp.float32
    )
    mixed = merge_heads(mixed.astype(jnp.bfloat16))
    return (widened + jnp.dot(mixed, w_out, preferred_element_type=jnp.float32)).astype(
        jnp.bfloat16
    )


def backward(tokens_in, upstream, gain_vec, w_in, w_out, layout):
    widened, inv_rms, queries, key_part, values, probs, probs_b, factor = recompute(
        tokens_in, gain_vec, w_in, layout
    )
    key_form = layout.replace("l", "m")
    d_mixed = jnp.dot(upstream, w_out.T, preferred_element_type=jnp.float32).astype(jnp.bfloat16)
    d_mixed = d_mixed.reshape(d_mixed.shape[:-1] + (H, d_mixed.shape[-1] // H))
    d_probs = jnp.einsum(
        layout + "," + key_form + "->bhlm", d_mixed, values, preferred_element_type=jnp.float32
    )
    d_values = jnp.einsum(
        "bhlm," + layout + "->" + key_form, probs_b, d_mixed, preferred_element_type=jnp.float32
    ).astype(jnp.bfloat16)
    centre = jnp.sum(probs * d_probs, axis=-1, keepdims=True)
    d_scores = (probs * (d_probs - centre) * factor).astype(jnp.bfloat16)
    d_queries = jnp.einsum(
        "bhlm," + key_form + "->" + layout, d_scores, key_part, preferred_element_type=jnp.float32
    ).astype(jnp.bfloat16)
    d_keys = jnp.einsum(
        "bhlm," + layout + "->" + key_form, d_scores, queries, preferred_element_type=jnp.float32
    ).astype(jnp.bfloat16)
    joined = jnp.concatenate(
        [merge_heads(d_queries), merge_heads(d_keys), merge_heads(d_values)], axis=-1
    )
    d_normed = jnp.dot(joined, w_in.T, preferred_element_type=jnp.float32)
    scaled = d_normed * gain_vec
    d_tokens = inv_rms * (
        scaled - widened * inv_rms * inv_rms * jnp.mean(scaled * widened, axis=-1, keepdims=True)
    )
    return (upstream.astype(jnp.float32) + d_tokens).astype(jnp.bfloat16)


def line_forward(lines, gain_vec, w_in, w_out):
    feature_count = lines.shape[3]
    flat = lines.reshape(-1, lines.shape[2], feature_count)
    return forward_out(flat, gain_vec, w_in, w_out, "blhe").reshape(lines.shape)


def line_backward(lines, upstream, gain_vec, w_in, w_out):
    feature_count = lines.shape[3]
    flat = lines.reshape(-1, lines.shape[2], feature_count)
    flat_up = upstream.reshape(flat.shape)
    return backward(flat, flat_up, gain_vec, w_in, w_out, "blhe").reshape(lines.shape)


def per_device(tokens, cotangent, gain_x, wqkv_x, wo_x, gain_z, wqkv_z, wo_z):
    full_in_x, full_out_x = (
        lax.all_gather(wqkv_x, "tr", axis=0, tiled=True),
        lax.all_gather(wo_x, "tr", axis=0, tiled=True),
    )
    full_in_z, full_out_z = (
        lax.all_gather(wqkv_z, "tr", axis=0, tiled=True),
        lax.all_gather(wo_z, "tr", axis=0, tiled=True),
    )
    width = tokens.shape[-1]
    lines = lax.all_to_all(tokens, "tr", split_axis=1, concat_axis=2, tiled=True)
    cot_lines = lax.all_to_all(cotangent, "tr", split_axis=1, concat_axis=2, tiled=True)
    cells = lines.shape[1] * lines.shape[2]
    flat = (lines.shape[0], cells, width)
    cot_columns = lax.all_to_all(
        cot_lines.reshape(flat), "gz", split_axis=1, concat_axis=0, tiled=True
    )
    mid_lines = line_forward(lines, gain_x, full_in_x, full_out_x)
    mid_columns = lax.all_to_all(
        mid_lines.reshape(flat), "gz", split_axis=1, concat_axis=0, tiled=True
    )
    grad_columns = backward(mid_columns, cot_columns, gain_z, full_in_z, full_out_z, "lbhe")
    grad_lines = lax.all_to_all(grad_columns, "gz", split_axis=0, concat_axis=1, tiled=True)
    result_lines = line_backward(
        lines, grad_lines.reshape(lines.shape), gain_x, full_in_x, full_out_x
    )
    return lax.all_to_all(result_lines, "tr", split_axis=2, concat_axis=1, tiled=True)


def solution(mesh):
    return jax.shard_map(
        per_device,
        mesh=mesh,
        in_specs=(
            P("gz", None, "tr", None),
            P("gz", None, "tr", None),
            P(),
            P("tr", None),
            P("tr", None),
            P(),
            P("tr", None),
            P("tr", None),
        ),
        out_specs=P("gz", None, "tr", None),
        check_vma=False,
    )
```

profile of v0, /device:TPU:0, one launch (start us, length us, event | category | flops | bytes accessed | tf_op | source)
XLA Modules:
  0.0 194.4 jit_solution(14103475853062895245)
XLA Ops:
  9.3 1.1 copy.114
  10.5 4.2 %all-to-all-start.2 = ((bf16[5,32,2,768]{3,2,0,1:T(2,128)(2,1)}), bf16[5,32,2,768]{3,2,0,1:T(2,128)(2,1)S(1)}, u32[]{:S(2)}, u32[]{:S(2)}) async-start(bf16[5,32,2,768]{3,2,0,1:T(2,128)(2,1)} %copy.114), calls=%async_computation.2 | async-start | bytes 983040 | tf_op jit(solution)/shard_map/all_to_all | solution.py:114
  15.8 9.2 %all-to-all-done.2 = bf16[5,32,2,768]{3,2,0,1:T(2,128)(2,1)S(1)} async-done(((bf16[5,32,2,768]{3,2,0,1:T(2,128)(2,1)}), bf16[5,32,2,768]{3,2,0,1:T(2,128)(2,1)S(1)}, u32[]{:S(2)}, u32[]{:S(2)}) %all-to-all-start.2) | async-done | bytes 491552 | tf_op jit(solution)/shard_map/all_to_all | solution.py:114
  25.0 3.5 %all-to-all-start = ((bf16[5,32,2,768]{3,2,0,1:T(2,128)(2,1)}), bf16[5,32,2,768]{3,2,0,1:T(2,128)(2,1)S(1)}, u32[]{:S(2)}, u32[]{:S(2)}) async-start(bf16[5,32,2,768]{3,2,0,1:T(2,128)(2,1)} %copy.109), calls=%async_computation | async-start | bytes 983040 | tf_op jit(solution)/shard_map/all_to_all | solution.py:115
  29.4 13.1 %all-to-all-done = bf16[5,32,2,768]{3,2,0,1:T(2,128)(2,1)S(1)} async-done(((bf16[5,32,2,768]{3,2,0,1:T(2,128)(2,1)}), bf16[5,32,2,768]{3,2,0,1:T(2,128)(2,1)S(1)}, u32[]{:S(2)}, u32[]{:S(2)}) %all-to-all-start) | async-done | bytes 491552 | tf_op jit(solution)/shard_map/all_to_all | solution.py:115
  43.5 7.3 %all-to-all-start.1 = ((bf16[5,64,768]{2,0,1:T(8,128)(2,1)}), bf16[5,64,768]{2,0,1:T(8,128)(2,1)S(1)}, u32[]{:S(2)}, u32[]{:S(2)}) async-start(bf16[5,64,768]{2,0,1:T(8,128)(2,1)} %bitcast.2), calls=%async_computation.1 | async-start | bytes 1572864 | tf_op jit(solution)/shard_map/all_to_all | solution.py:118
  51.9 3.4 %convolution_convert_fusion.1 = bf16[40,8,2304]{2,1,0:T(8,128)(2,1)S(1)} fusion(bf16[768,2304]{1,0:T(8,128)(2,1)} %all-gather.5.cloned.1.call-done, f32[40,8,768]{2,1,0:T(8,128)S(1)} %reshape.140, f32[768]{0:T(1024)S(1)} %copy-done.8, f32[40,8]{1,0:T(8,128)S(1)} %copy.119), kind=kOutput, calls=%fused_computation.5 | convolution fusion | flops 1133936640 | bytes 6000896 | tf_op jit(solution)/shard_map/dot_general | solution.py:25
  55.3 1.8 fusion.105
  57.1 11.9 %all-gather.7.cloned.1.call-done = bf16[768,768]{1,0:T(8,128)(2,1)} async-done(((bf16[192,768]{1,0:T(8,128)(2,1)}), bf16[768,768]{1,0:T(8,128)(2,1)}) %all-gather.7.cloned.1.call-update) | async-done | bytes 1179664 | tf_op jit(solution)/shard_map/all_gather | solution.py:107
  69.0 2.6 %fusion.40 = bf16[40,8,768]{2,1,0:T(8,128)(2,1)S(1)} fusion(f32[40,8,768]{2,1,0:T(8,128)S(1)} %reshape.140, bf16[768,768]{1,0:T(8,128)(2,1)} %all-gather.7.cloned.1.call-done, bf16[40,8,2304]{2,1,0:T(8,128)(2,1)} %copy-done.5, f32[40,6,8,8]{2,3,1,0:T(8,128)} %get-tuple-element.9, f32[40,6,8]{2,1,0:T(8,128)S(1)} %get-tuple-element.8), kind=kOutput, calls=%fused_computation.38 | convolution fusion | flops 382187520 | bytes 4136448 | tf_op jit(solution)/shard_map/dot_general | solution.py:54
  71.7 1.2 copy.121
  72.9 5.5 %all-to-all-start.3 = ((bf16[5,64,768]{2,0,1:T(8,128)(2,1)}), bf16[5,64,768]{2,0,1:T(8,128)(2,1)S(1)}, u32[]{:S(2)}, u32[]{:S(2)}) async-start(bf16[5,64,768]{2,0,1:T(8,128)(2,1)} %copy.121), calls=%async_computation.3 | async-start | bytes 1572864 | tf_op jit(solution)/shard_map/all_to_all | solution.py:122
  78.5 9.5 %all-gather.11.cloned.1.call-done = bf16[768,768]{1,0:T(8,128)(2,1)} async-done(((bf16[192,768]{1,0:T(8,128)(2,1)}), bf16[768,768]{1,0:T(8,128)(2,1)}) %all-gather.11.cloned.1.call-update) | async-done | bytes 1179664 | tf_op jit(solution)/shard_map/all_gather | solution.py:111
  88.1 2.6 %fusion.43 = bf16[40,8,6,128]{3,1,2,0:T(8,128)(2,1)} fusion(bf16[40,8,768]{2,1,0:T(8,128)(2,1)S(1)} %bitcast.138, bf16[768,768]{1,0:T(8,128)(2,1)} %all-gather.11.cloned.1.call-done), kind=kOutput, calls=%fused_computation.50 | convolution fusion | flops 377733120 | bytes 2162688 | tf_op jit(solution)/shard_map/dot_general | solution.py:64
  90.7 8.3 %all-to-all-done.3 = bf16[5,64,768]{2,0,1:T(8,128)(2,1)S(1)} async-done(((bf16[5,64,768]{2,0,1:T(8,128)(2,1)}), bf16[5,64,768]{2,0,1:T(8,128)(2,1)S(1)}, u32[]{:S(2)}, u32[]{:S(2)}) %all-to-all-start.3) | async-done | bytes 491552 | tf_op jit(solution)/shard_map/all_to_all | solution.py:122
  99.6 20.7 %all-gather.9.cloned.1.call-done = bf16[768,2304]{1,0:T(8,128)(2,1)} async-done(((bf16[192,2304]{1,0:T(8,128)(2,1)}), bf16[768,2304]{1,0:T(8,128)(2,1)}) %all-gather.9.cloned.1.call-update) | async-done | bytes 3538960 | tf_op jit(solution)/shard_map/all_gather | solution.py:110
  120.3 3.3 %convolution_convert_fusion = bf16[40,8,2304]{2,1,0:T(8,128)(2,1)S(1)} fusion(bf16[768,2304]{1,0:T(8,128)(2,1)} %all-gather.9.cloned.1.call-done, f32[40,8,768]{2,1,0:T(8,128)S(1)} %bitcast.135, f32[768]{0:T(1024)S(1)} %copy-done.7, f32[40,8]{1,0:T(8,128)S(1)} %reshape.158), kind=kOutput, calls=%fused_computation.4 | convolution fusion | flops 1133936640 | bytes 6000896 | tf_op jit(solution)/shard_map/dot_general | solution.py:25
  125.2 2.6 %fusion.106 = (f32[8,6,40]{2,1,0:T(8,128)S(1)}, f32[8,6,40,40]{2,3,1,0:T(8,128)}) fusion(bf16[40,8,6,128]{3,1,2,0:T(8,128)(2,1)S(1)} %get-tuple-element.7, bf16[40,8,6,128]{3,1,2,0:T(8,128)(2,1)} %get-tuple-element.6), kind=kOutput, calls=%fused_computation.123 | convolution fusion | flops 19891240 | bytes 1297920 | tf_op jit(solution)/shard_map/sub | solution.py:40
  127.8 2.6 %fusion.48 = bf16[40,8,6,128]{3,0,2,1:T(8,128)(2,1)} fusion(bf16[40,8,6,128]{3,1,2,0:T(8,128)(2,1)} %fusion.43, f32[8,6,40,40]{2,3,1,0:T(8,128)} %get-tuple-element.11, f32[8,6,40]{2,1,0:T(8,128)S(1)} %get-tuple-element.10), kind=kOutput, calls=%fused_computation.55 | convolution fusion | flops 20060160 | bytes 1297920 | tf_op jit(solution)/shard_map/bhlm,lbhe->mbhe/dot_general | solution.py:69
  130.3 3.0 %fusion.47 = bf16[40,8,6,128]{3,0,2,1:T(8,128)(2,1)} fusion(f32[8,6,40,40]{2,3,1,0:T(8,128)S(1)} %fusion.60, bf16[40,8,6,128]{3,1,2,0:T(8,128)(2,1)} %get-tuple-element.6, f32[8,6,40,40]{2,3,1,0:T(8,128)} %get-tuple-element.11, f32[8,6,40]{2,1,0:T(8,128)S(1)} %get-tuple-element.10), kind=kOutput, calls=%fused_computation.54 | convolution fusion | flops 20446120 | bytes 1605120 | tf_op jit(solution)/shard_map/bhlm,lbhe->mbhe/dot_general | solution.py:77
  133.3 2.9 %fusion.46 = bf16[40,8,6,128]{3,0,2,1:T(8,128)(2,1)} fusion(f32[8,6,40,40]{2,3,1,0:T(8,128)S(1)} %fusion.60, bf16[40,8,6,128]{3,1,2,0:T(8,128)(2,1)S(1)} %get-tuple-element.7, f32[8,6,40,40]{2,3,1,0:T(8,128)} %get-tuple-element.11, f32[8,6,40]{2,1,0:T(8,128)S(1)} %get-tuple-element.10), kind=kOutput, calls=%fused_computation.53 | convolution fusion | flops 20446120 | bytes 1605120 | tf_op jit(solution)/shard_map/bhlm,mbhe->lbhe/dot_general | solution.py:74
  136.3 1.2 copy.183
  137.4 1.4 copy_bitcast_fusion.1
  138.8 3.5 %multiply_reduce_fusion.3 = (f32[40,8]{1,0:T(8,128)S(1)}, f32[40,8,768]{2,1,0:T(8,128)S(1)}) fusion(f32[40,8,768]{2,1,0:T(8,128)S(1)} %bitcast.136, f32[768]{0:T(1024)S(1)} %copy-done.7, bf16[768,2304]{1,0:T(8,128)(2,1)} %all-gather.9.cloned.1.call-done, bf16[40,8,768]{2,1,0:T(8,128)(2,1)S(1)} %get-tuple-element.16, ...), kind=kOutput, calls=%fused_computation.69 | convolution fusion | flops 1137622784 | bytes 6983936 | tf_op jit(solution)/shard_map/dot_general | solution.py:83
  142.6 19.6 %all_to_all.84 = bf16[40,8,768]{2,1,0:T(8,128)(2,1)S(1)} all-to-all(bf16[40,8,768]{2,1,0:T(8,128)(2,1)S(1)} %add_convert_fusion.1), channel_id=1, replica_groups=mesh['tr'=4,'gz'=8] {'gz'}, dimensions={0} | all-to-all | bytes 983040 | tf_op jit(solution)/shard_map/all_to_all | solution.py:126
  163.5 1.2 fusion.51
  164.7 1.5 fusion.79
  166.2 2.7 %fusion.49 = bf16[40,8,768]{2,1,0:T(8,128)(2,1)} fusion(f32[40,6,8,8]{2,3,1,0:T(8,128)S(1)} %fusion.79, bf16[40,8,2304]{2,1,0:T(8,128)(2,1)} %copy-done.5, f32[40,6,8,8]{2,3,1,0:T(8,128)S(1)} %copy-done.10, f32[40,6,8]{2,1,0:T(8,128)} %copy-done.11), kind=kOutput, calls=%fused_computation.56 | convolution fusion | flops 4287367 | bytes 5242880 | tf_op jit(solution)/shard_map/bhlm,bmhe->blhe/dot_general | solution.py:74
  168.9 2.6 %fusion.50 = bf16[40,8,768]{2,1,0:T(8,128)(2,1)} fusion(f32[40,6,8,8]{2,3,1,0:T(8,128)S(1)} %fusion.79, bf16[40,8,2304]{2,1,0:T(8,128)(2,1)} %copy-done.5, f32[40,6,8,8]{2,3,1,0:T(8,128)S(1)} %copy-done.10, f32[40,6,8]{2,1,0:T(8,128)} %copy-done.11), kind=kOutput, calls=%fused_computation.57 | convolution fusion | flops 4287367 | bytes 5242880 | tf_op jit(solution)/shard_map/bhlm,blhe->bmhe/dot_general | solution.py:77
  171.5 3.9 %multiply_reduce_fusion.2 = (f32[40,8]{1,0:T(8,128)S(1)}, f32[40,8,768]{2,1,0:T(8,128)S(1)}) fusion(f32[40,8,768]{2,1,0:T(8,128)S(1)} %reshape.140, f32[768]{0:T(1024)S(1)} %copy-done.8, bf16[768,2304]{1,0:T(8,128)(2,1)} %all-gather.5.cloned.1.call-done, bf16[40,8,768]{2,1,0:T(8,128)(2,1)} %fusion.51, bf16[40,8,768]{2,1,0:T(8,128)(2,1)} %fusion.50, ...), kind=kOutput, calls=%fused_computation.67 | convolution fusion | flops 1137622784 | bytes 6983936 | tf_op jit(solution)/shard_map/dot_general | solution.py:83
  175.9 10.9 %all_to_all.85 = bf16[5,8,8,768]{3,1,0,2:T(8,128)(2,1)S(1)} all-to-all(bf16[5,8,8,768]{3,1,0,2:T(8,128)(2,1)S(1)} %copy.139), channel_id=1, replica_groups=mesh['tr'=4,'gz'=8] {'tr'}, dimensions={2} | all-to-all | bytes 983040 | tf_op jit(solution)/shard_map/all_to_all | solution.py:130
  186.7 1.2 copy.140
  (63 shorter events, 11.0 us)
Async XLA Ops:
  6.5 2.8 %copy-start.2 = (bf16[5,32,2,768]{3,2,1,0:T(2,128)(2,1)S(1)}, bf16[5,32,2,768]{3,2,1,0:T(2,128)(2,1)}, u32[]{:S(2)}) copy-start(bf16[5,32,2,768]{3,2,1,0:T(2,128)(2,1)} %param.8) | copy-start | bytes 1474564
  6.5 45.4 %all-gather.5.cloned.1.call-start = ((), (), s32[]{:S(2)}) async-start(), calls=%async_computation.6 | async-start | bytes 4423680 | tf_op jit(solution)/shard_map/all_gather | solution.py:106
  7.3 61.8 %all-gather.7.cloned.1.call-start = ((), (), s32[]{:S(2)}) async-start(), calls=%async_computation.7 | async-start | bytes 1474560 | tf_op jit(solution)/shard_map/all_gather | solution.py:107
  8.0 80.1 %all-gather.11.cloned.1.call-start = ((), (), s32[]{:S(2)}) async-start(), calls=%async_computation.9 | async-start | bytes 1474560 | tf_op jit(solution)/shard_map/all_gather | solution.py:111
  8.7 5.9 %copy-start.3 = (bf16[5,32,2,768]{3,2,1,0:T(2,128)(2,1)S(1)}, bf16[5,32,2,768]{3,2,1,0:T(2,128)(2,1)}, u32[]{:S(2)}) copy-start(bf16[5,32,2,768]{3,2,1,0:T(2,128)(2,1)} %param.9) | copy-start | bytes 1474564
  8.8 111.5 %all-gather.9.cloned.1.call-start = ((), (), s32[]{:S(2)}) async-start(), calls=%async_computation.8 | async-start | bytes 4423680 | tf_op jit(solution)/shard_map/all_gather | solution.py:110
  10.5 14.5 %all-to-all-start.2 = ((bf16[5,32,2,768]{3,2,0,1:T(2,128)(2,1)}), bf16[5,32,2,768]{3,2,0,1:T(2,128)(2,1)S(1)}, u32[]{:S(2)}, u32[]{:S(2)}) async-start(bf16[5,32,2,768]{3,2,0,1:T(2,128)(2,1)} %copy.114), calls=%async_computation.2 | async-start | bytes 983040 | tf_op jit(solution)/shard_map/all_to_all | solution.py:114
  25.0 17.5 %all-to-all-start = ((bf16[5,32,2,768]{3,2,0,1:T(2,128)(2,1)}), bf16[5,32,2,768]{3,2,0,1:T(2,128)(2,1)S(1)}, u32[]{:S(2)}, u32[]{:S(2)}) async-start(bf16[5,32,2,768]{3,2,0,1:T(2,128)(2,1)} %copy.109), calls=%async_computation | async-start | bytes 983040 | tf_op jit(solution)/shard_map/all_to_all | solution.py:115
  43.5 29.4 %all-to-all-start.1 = ((bf16[5,64,768]{2,0,1:T(8,128)(2,1)}), bf16[5,64,768]{2,0,1:T(8,128)(2,1)S(1)}, u32[]{:S(2)}, u32[]{:S(2)}) async-start(bf16[5,64,768]{2,0,1:T(8,128)(2,1)} %bitcast.2), calls=%async_computation.1 | async-start | bytes 1572864 | tf_op jit(solution)/shard_map/all_to_all | solution.py:118
  50.8 1.1 copy-start.8
  55.3 1.8 copy-start.5
  57.1 14.6 %copy-start.11 = (f32[40,6,8]{2,1,0:T(8,128)}, f32[40,6,8]{2,1,0:T(8,128)S(1)}, u32[]{:S(2)}) copy-start(f32[40,6,8]{2,1,0:T(8,128)S(1)} %get-tuple-element.8) | copy-start | bytes 23044
  72.9 26.1 %all-to-all-start.3 = ((bf16[5,64,768]{2,0,1:T(8,128)(2,1)}), bf16[5,64,768]{2,0,1:T(8,128)(2,1)S(1)}, u32[]{:S(2)}, u32[]{:S(2)}) async-start(bf16[5,64,768]{2,0,1:T(8,128)(2,1)} %copy.121), calls=%async_computation.3 | async-start | bytes 1572864 | tf_op jit(solution)/shard_map/all_to_all | solution.py:122
  78.5 20.7 %copy-start = (bf16[8,5,8,768]{3,2,1,0:T(8,128)(2,1)}, bf16[8,5,8,768]{3,2,1,0:T(8,128)(2,1)S(1)}, u32[]{:S(2)}) copy-start(bf16[8,5,8,768]{3,2,1,0:T(8,128)(2,1)S(1)} %copy.113) | copy-start | bytes 1474564
  90.7 29.6 %copy-start.7 = (f32[768]{0:T(1024)S(1)}, f32[768]{0:T(1024)}, u32[]{:S(2)}) copy-start(f32[768]{0:T(1024)} %param.13) | copy-start | bytes 9220
  123.7 1.1 copy-start.4
  138.8 3.5 %copy-start.1 = (bf16[8,5,8,768]{3,2,1,0:T(8,128)(2,1)S(1)}, bf16[8,5,8,768]{3,2,1,0:T(8,128)(2,1)}, u32[]{:S(2)}) copy-start(bf16[8,5,8,768]{3,2,1,0:T(8,128)(2,1)} %copy-done) | copy-start | bytes 1474564
  142.6 19.7 %copy-start.6 = (bf16[768,768]{1,0:T(8,128)(2,1)S(1)}, bf16[768,768]{1,0:T(8,128)(2,1)}, u32[]{:S(2)}) copy-start(bf16[768,768]{1,0:T(8,128)(2,1)} %all-gather.7.cloned.1.call-done) | copy-start | bytes 3538948
  162.3 1.2 copy-start.9
  162.3 1.2 copy-start.12
  164.7 1.5 copy-start.10
Sparse Core Ops, SparseCore 0:
  8.9 40.0 all-gather.4
  50.5 18.4 all-gather.6
  70.6 17.4 all-gather.10
  89.5 30.7 all-gather.8
where the time goes:
time: 195 us; the launch traced here: 194 us
  waiting for transfers between devices  75.3 us (39%)
  matrix products  41.2 us (21%)
  blocking collectives  30.5 us (16%)
  starting transfers between devices  20.6 us (11%)
  between operations  13.4 us (7%)
  local copies, waits for them, and re-layouts  11.4 us (6%)
    all_gather x1, waiting for transfers between devices, per_device(): lax.all_gather(wqkv_z, 'tr', axis=0, tiled=True)  20.7 us
    all_to_all x1, blocking collectives, per_device(): lax.all_to_all(grad_columns, 'gz', split_axis=0, concat_axis=1, tiled=True)  19.6 us
    all_to_all x1, waiting for transfers between devices, per_device(): lax.all_to_all(cotangent, 'tr', split_axis=1, concat_axis=2, tiled=True)  13.1 us
    all_gather x1, waiting for transfers between devices, per_device(): lax.all_gather(wo_x, 'tr', axis=0, tiled=True)  11.9 us
    all_to_all x1, blocking collectives, per_device(): lax.all_to_all(result_lines, 'tr', split_axis=2, concat_axis=1, tiled=True)  10.9 us
    all_gather x1, waiting for transfers between devices, per_device(): lax.all_gather(wo_z, 'tr', axis=0, tiled=True)  9.53 us
    all_to_all x1, waiting for transfers between devices, per_device(): lax.all_to_all(tokens, 'tr', split_axis=1, concat_axis=2, tiled=True)  9.19 us
    all_to_all x1, waiting for transfers between devices, per_device(): lax.all_to_all(mid_lines.reshape(flat), 'gz', split_axis=1, concat_axis=0...  8.26 us
  transfers between devices with their start and end apart: 8, of which 6 were waited for; matrix products, arithmetic and copies ran while one was open for 9% of the time, Pallas kernels for 0%

commit v1 on v0

--- a/solution.py
+++ b/solution.py
@@ -3,6 +3,7 @@
 import jax.numpy as jnp
 from jax import lax
 from jax.sharding import PartitionSpec as P
+from jax.lax import axis_index, ppermute, psum
 
 H = 6
 
@@ -106,8 +107,35 @@
         lax.all_gather(wqkv_x, "tr", axis=0, tiled=True),
         lax.all_gather(wo_x, "tr", axis=0, tiled=True),
     )
+
+    def enter_corner_in(tile_in, which_axis):
+        u1 = psum(1, which_axis)
+        extra, prior, v_now = (u1, axis_index(which_axis), tile_in.shape[0])
+        upper = out_arr = tile_in
+        frame_out = lax.dynamic_update_slice_in_dim(
+            jnp.zeros(
+                [kk * extra if b == 0 else kk for b, kk in enumerate(tile_in.shape)], tile_in.dtype
+            ),
+            tile_in,
+            prior * v_now,
+            axis=0,
+        )
+        for idx in range(1, extra // 2 + 1):
+            upper = ppermute(upper, which_axis, [(b, (b + 1) % extra) for b in range(extra)])
+            frame_out = lax.dynamic_update_slice_in_dim(
+                frame_out, upper, (prior - idx) % extra * v_now, axis=0
+            )
+            if 2 * idx < extra:
+                out_arr = ppermute(
+                    out_arr, which_axis, [(b, (b - 1) % extra) for b in range(extra)]
+                )
+                frame_out = lax.dynamic_update_slice_in_dim(
+                    frame_out, out_arr, (prior + idx) % extra * v_now, axis=0
+                )
+        return frame_out
+
     full_in_z, full_out_z = (
-        lax.all_gather(wqkv_z, "tr", axis=0, tiled=True),
+        enter_corner_in(wqkv_z, "tr"),
         lax.all_gather(wo_z, "tr", axis=0, tiled=True),
     )
     width = tokens.shape[-1]

time: 195 us -> 188 us (0.964)
  waiting for transfers between devices: 75.3 us -> 60.7 us
  local copies, waits for them, and re-layouts: 11.4 us -> 19.7 us
  blocking collectives: 30.5 us -> 28.3 us
    all_to_all x1, waiting for transfers between devices: 9.19 us -> 31.8 us  [per_device(): lax.all_to_all(tokens, 'tr', split_axis=1, concat_axis=2, tiled=True)]
    all_gather x1 -> x0, waiting for transfers between devices: 20.7 us -> none  [per_device(): lax.all_gather(wqkv_z, 'tr', axis=0, tiled=True)]
    all_gather x1, waiting for transfers between devices: 11.9 us -> 0.02 us  [per_device(): lax.all_gather(wo_x, 'tr', axis=0, tiled=True)]
    all_gather x1, waiting for transfers between devices: 9.53 us -> 0.02 us  [per_device(): lax.all_gather(wo_z, 'tr', axis=0, tiled=True)]
    dynamic_update_slice x0 -> x4, local copies, waits for them, and re-layouts: none -> 7.48 us  [the longest x2 4.33 us: enter_corner_in(): lax.dynamic_update_slice_in_dim(frame_out, upper, (prior - idx) % extra *...]
    all_to_all x1, waiting for transfers between devices: 0.01 us -> 7.32 us  [per_device(): lax.all_to_all(cot_lines.reshape(flat), 'gz', split_axis=1, concat_axis=0...]
    all_to_all x1, waiting for transfers between devices: 13.1 us -> 6.43 us  [per_device(): lax.all_to_all(cotangent, 'tr', split_axis=1, concat_axis=2, tiled=True)]
    all_to_all x1, waiting for transfers between devices: 8.26 us -> 13 us  [per_device(): lax.all_to_all(mid_lines.reshape(flat), 'gz', split_axis=1, concat_axis=0...]
  transfers between devices with their start and end apart: 8 -> 10, of which waited for: 6 -> 4; matrix products, arithmetic and copies ran while one was open for 9% -> 16% of each run, Pallas kernels for 0% -> 0%
where the time goes in v1:
time: 188 us; the launch traced here: 187 us
  waiting for transfers between devices  60.7 us (32%)
  matrix products  42.4 us (23%)
  blocking collectives  28.3 us (15%)
  starting transfers between devices  20.4 us (11%)
  local copies, waits for them, and re-layouts  19.7 us (10%)
  between operations  13.5 us (7%)
  other arithmetic  1.89 us (1%)
    all_to_all x1, waiting for transfers between devices, per_device(): lax.all_to_all(tokens, 'tr', split_axis=1, concat_axis=2, tiled=True)  31.8 us
    all_to_all x1, blocking collectives, per_device(): lax.all_to_all(grad_columns, 'gz', split_axis=0, concat_axis=1, tiled=True)  17.5 us
    all_to_all x1, waiting for transfers between devices, per_device(): lax.all_to_all(mid_lines.reshape(flat), 'gz', split_axis=1, concat_axis=0...  13 us
    all_to_all x1, blocking collectives, per_device(): lax.all_to_all(result_lines, 'tr', split_axis=2, concat_axis=1, tiled=True)  10.9 us
    dot_general x2, matrix products, recompute(): jnp.dot(normed, w_in, preferred_element_type=jnp.float32)  7.87 us
    all_to_all x1, waiting for transfers between devices, per_device(): lax.all_to_all(cot_lines.reshape(flat), 'gz', split_axis=1, concat_axis=0...  7.32 us
    all_to_all x1, starting transfers between devices, per_device(): lax.all_to_all(cot_lines.reshape(flat), 'gz', split_axis=1, concat_axis=0...  7.09 us
    all_to_all x1, waiting for transfers between devices, per_device(): lax.all_to_all(cotangent, 'tr', split_axis=1, concat_axis=2, tiled=True)  6.43 us
  transfers between devices with their start and end apart: 10, of which 4 were waited for; matrix products, arithmetic and copies ran while one was open for 16% of the time, Pallas kernels for 0%

profile of v1, /device:TPU:0, one launch (start us, length us, event | category | flops | bytes accessed | tf_op | source)
XLA Modules:
  0.0 186.9 jit_solution(5418886847737771807)
XLA Ops:
  8.5 2.0 %collective-permute-start.1 = (bf16[192,2304]{1,0:T(8,128)(2,1)}, bf16[192,2304]{1,0:T(8,128)(2,1)}, u32[]{:S(2)}, u32[]{:S(2)}) collective-permute-start(bf16[192,2304]{1,0:T(8,128)(2,1)} %param.14), channel_id=1, source_target_pairs={{0,24},{8,0},{16,8},{24,16},{1,25},{9,1},{17,9},{25,17},{2,26},{10... | collective-permute-start | bytes 2654216 | tf_op jit(solution)/shard_map/ppermute | solution.py:129
  10.5 2.1 %copy.114 = bf16[5,32,2,768]{3,2,0,1:T(2,128)(2,1)} copy(bf16[5,32,2,768]{3,2,1,0:T(2,128)(2,1)} %param.8) | data formatting | bytes 983040 | tf_op args[0]
  12.7 3.5 %all-to-all-start.2 = ((bf16[5,32,2,768]{3,2,0,1:T(2,128)(2,1)}), bf16[5,32,2,768]{3,2,0,1:T(2,128)(2,1)S(1)}, u32[]{:S(2)}, u32[]{:S(2)}) async-start(bf16[5,32,2,768]{3,2,0,1:T(2,128)(2,1)} %copy.114), calls=%async_computation.2 | async-start | bytes 983040 | tf_op jit(solution)/shard_map/all_to_all | solution.py:142
  18.1 2.0 %broadcast_in_dim.2 = bf16[768,2304]{1,0:T(8,128)(2,1)} broadcast(bf16[]{:T(256)} %constant.45.clone.1), dimensions={} | broadcast | bytes 3538946 | tf_op jit(solution)/shard_map/broadcast_in_dim | solution.py:116
  21.1 31.8 %all-to-all-done.2 = bf16[5,32,2,768]{3,2,0,1:T(2,128)(2,1)S(1)} async-done(((bf16[5,32,2,768]{3,2,0,1:T(2,128)(2,1)}), bf16[5,32,2,768]{3,2,0,1:T(2,128)(2,1)S(1)}, u32[]{:S(2)}, u32[]{:S(2)}) %all-to-all-start.2) | async-done | bytes 491552 | tf_op jit(solution)/shard_map/all_to_all | solution.py:142
  52.9 3.5 %all-to-all-start = ((bf16[5,32,2,768]{3,2,0,1:T(2,128)(2,1)}), bf16[5,32,2,768]{3,2,0,1:T(2,128)(2,1)S(1)}, u32[]{:S(2)}, u32[]{:S(2)}) async-start(bf16[5,32,2,768]{3,2,0,1:T(2,128)(2,1)} %copy.109), calls=%async_computation | async-start | bytes 983040 | tf_op jit(solution)/shard_map/all_to_all | solution.py:143
  58.4 6.4 %all-to-all-done = bf16[5,32,2,768]{3,2,0,1:T(2,128)(2,1)S(1)} async-done(((bf16[5,32,2,768]{3,2,0,1:T(2,128)(2,1)}), bf16[5,32,2,768]{3,2,0,1:T(2,128)(2,1)S(1)}, u32[]{:S(2)}, u32[]{:S(2)}) %all-to-all-start) | async-done | bytes 491552 | tf_op jit(solution)/shard_map/all_to_all | solution.py:143
  65.9 7.1 %all-to-all-start.1 = ((bf16[5,64,768]{2,0,1:T(8,128)(2,1)}), bf16[5,64,768]{2,0,1:T(8,128)(2,1)S(1)}, u32[]{:S(2)}, u32[]{:S(2)}) async-start(bf16[5,64,768]{2,0,1:T(8,128)(2,1)} %bitcast.2), calls=%async_computation.1 | async-start | bytes 1572864 | tf_op jit(solution)/shard_map/all_to_all | solution.py:146
  73.0 2.1 %constant_dynamic-update-slice_fusion.2 = bf16[768,2304]{1,0:T(8,128)(2,1)} fusion(bf16[768,2304]{1,0:T(8,128)(2,1)} %constant_dynamic-update-slice_fusion.3, bf16[192,2304]{1,0:T(8,128)(2,1)} %collective-permute-done, s32[]{:T(128)S(6)} %select_n.29), kind=kLoop, calls=%fused_computation.110 | loop fusion | bytes 1769476 | tf_op jit(solution)/shard_map/dynamic_update_slice | solution.py:125
  75.2 4.5 %convolution_convert_fusion.1 = bf16[40,8,2304]{2,1,0:T(8,128)(2,1)} fusion(bf16[768,2304]{1,0:T(8,128)(2,1)} %all-gather.4.cloned.1.call-done, f32[40,8,768]{2,1,0:T(8,128)S(1)} %reshape.140, f32[768]{0:T(1024)S(1)} %copy-done.8, f32[40,8]{1,0:T(8,128)S(1)} %copy.119), kind=kOutput, calls=%fused_computation.5 | convolution fusion | flops 1133936640 | bytes 6000896 | tf_op jit(solution)/shard_map/dot_general | solution.py:26
  79.7 2.0 %fusion.105 = (f32[40,6,8]{2,1,0:T(8,128)S(1)}, f32[40,6,8,8]{2,3,1,0:T(8,128)S(1)}) fusion(bf16[40,8,2304]{2,1,0:T(8,128)(2,1)} %convolution_convert_fusion.1), kind=kOutput, calls=%fused_computation.126 | convolution fusion | flops 3978247 | bytes 1052160 | tf_op jit(solution)/shard_map/sub | solution.py:41
  81.7 2.7 %fusion.40 = bf16[40,8,768]{2,1,0:T(8,128)(2,1)S(1)} fusion(f32[40,8,768]{2,1,0:T(8,128)S(1)} %reshape.140, bf16[768,768]{1,0:T(8,128)(2,1)} %all-gather.6.cloned.1.call-done, bf16[40,8,2304]{2,1,0:T(8,128)(2,1)} %convolution_convert_fusion.1, f32[40,6,8,8]{2,3,1,0:T(8,128)S(1)} %get-tuple-element.9, f32[40,6,8]{2,1,0:T(8,128)S(1)} %get-tuple-element.8), kind=kOutput, calls=%fused_computation.38 | convolution fusion | flops 382187520 | bytes 3214848 | tf_op jit(solution)/shard_map/dot_general | solution.py:55
  84.5 1.2 copy.121
  85.7 7.3 %all-to-all-done.1 = bf16[5,64,768]{2,0,1:T(8,128)(2,1)S(1)} async-done(((bf16[5,64,768]{2,0,1:T(8,128)(2,1)}), bf16[5,64,768]{2,0,1:T(8,128)(2,1)S(1)}, u32[]{:S(2)}, u32[]{:S(2)}) %all-to-all-start.1) | async-done | bytes 491552 | tf_op jit(solution)/shard_map/all_to_all | solution.py:146
  93.0 3.7 %all-to-all-start.3 = ((bf16[5,64,768]{2,0,1:T(8,128)(2,1)}), bf16[5,64,768]{2,0,1:T(8,128)(2,1)S(1)}, u32[]{:S(2)}, u32[]{:S(2)}) async-start(bf16[5,64,768]{2,0,1:T(8,128)(2,1)} %copy.121), calls=%async_computation.3 | async-start | bytes 1572864 | tf_op jit(solution)/shard_map/all_to_all | solution.py:150
  96.7 2.1 %constant_dynamic-update-slice_fusion.1 = bf16[768,2304]{1,0:T(8,128)(2,1)} fusion(bf16[768,2304]{1,0:T(8,128)(2,1)} %constant_dynamic-update-slice_fusion.2, bf16[192,2304]{1,0:T(8,128)(2,1)} %collective-permute-done.1, s32[]{:T(128)S(6)} %select_n.31), kind=kLoop, calls=%fused_computation.109 | loop fusion | bytes 1769476 | tf_op jit(solution)/shard_map/dynamic_update_slice | solution.py:132
  99.0 2.6 %fusion.43 = bf16[40,8,6,128]{3,1,2,0:T(8,128)(2,1)} fusion(bf16[40,8,768]{2,1,0:T(8,128)(2,1)S(1)} %bitcast.138, bf16[768,768]{1,0:T(8,128)(2,1)} %all-gather.8.cloned.1.call-done), kind=kOutput, calls=%fused_computation.50 | convolution fusion | flops 377733120 | bytes 2162688 | tf_op jit(solution)/shard_map/dot_general | solution.py:65
  101.7 2.2 %constant_dynamic-update-slice_fusion = bf16[768,2304]{1,0:T(8,128)(2,1)} fusion(bf16[768,2304]{1,0:T(8,128)(2,1)} %constant_dynamic-update-slice_fusion.1, bf16[192,2304]{1,0:T(8,128)(2,1)} %collective-permute-done.2, s32[]{:T(128)S(6)} %select_n.33), kind=kLoop, calls=%fused_computation.108 | loop fusion | bytes 1769476 | tf_op jit(solution)/shard_map/dynamic_update_slice | solution.py:125
  103.9 13.0 %all-to-all-done.3 = bf16[5,64,768]{2,0,1:T(8,128)(2,1)S(1)} async-done(((bf16[5,64,768]{2,0,1:T(8,128)(2,1)}), bf16[5,64,768]{2,0,1:T(8,128)(2,1)S(1)}, u32[]{:S(2)}, u32[]{:S(2)}) %all-to-all-start.3) | async-done | bytes 491552 | tf_op jit(solution)/shard_map/all_to_all | solution.py:150
  117.5 3.4 %convolution_convert_fusion = bf16[40,8,2304]{2,1,0:T(8,128)(2,1)S(1)} fusion(bf16[768,2304]{1,0:T(8,128)(2,1)} %constant_dynamic-update-slice_fusion, f32[40,8,768]{2,1,0:T(8,128)S(1)} %bitcast.135, f32[768]{0:T(1024)S(1)} %copy-done.7, f32[40,8]{1,0:T(8,128)S(1)} %reshape.158), kind=kOutput, calls=%fused_computation.4 | convolution fusion | flops 1133936640 | bytes 6000896 | tf_op jit(solution)/shard_map/dot_general | solution.py:26
  122.4 2.8 %fusion.106 = (f32[8,6,40]{2,1,0:T(8,128)S(1)}, f32[8,6,40,40]{2,3,1,0:T(8,128)}) fusion(bf16[40,8,6,128]{3,1,2,0:T(8,128)(2,1)} %get-tuple-element.7, bf16[40,8,6,128]{3,1,2,0:T(8,128)(2,1)} %get-tuple-element.6), kind=kOutput, calls=%fused_computation.127 | convolution fusion | flops 19891240 | bytes 1297920 | tf_op jit(solution)/shard_map/sub | solution.py:41
  125.1 3.1 %fusion.46 = bf16[40,8,6,128]{3,0,2,1:T(8,128)(2,1)} fusion(f32[8,6,40,40]{2,3,1,0:T(8,128)S(1)} %fusion.60, bf16[40,8,6,128]{3,1,2,0:T(8,128)(2,1)} %get-tuple-element.7, f32[8,6,40,40]{2,3,1,0:T(8,128)} %get-tuple-element.11, f32[8,6,40]{2,1,0:T(8,128)S(1)} %get-tuple-element.10), kind=kOutput, calls=%fused_computation.53 | convolution fusion | flops 20446120 | bytes 1605120 | tf_op jit(solution)/shard_map/bhlm,mbhe->lbhe/dot_general | solution.py:75
  128.2 3.0 %fusion.47 = bf16[40,8,6,128]{3,0,2,1:T(8,128)(2,1)} fusion(f32[8,6,40,40]{2,3,1,0:T(8,128)S(1)} %fusion.60, bf16[40,8,6,128]{3,1,2,0:T(8,128)(2,1)} %get-tuple-element.6, f32[8,6,40,40]{2,3,1,0:T(8,128)} %get-tuple-element.11, f32[8,6,40]{2,1,0:T(8,128)S(1)} %get-tuple-element.10), kind=kOutput, calls=%fused_computation.54 | convolution fusion | flops 20446120 | bytes 1605120 | tf_op jit(solution)/shard_map/bhlm,lbhe->mbhe/dot_general | solution.py:78
  131.2 1.8 fusion.48
  133.4 3.4 %multiply_reduce_fusion.3 = (f32[40,8]{1,0:T(8,128)S(1)}, f32[40,8,768]{2,1,0:T(8,128)S(1)}) fusion(f32[40,8,768]{2,1,0:T(8,128)S(1)} %bitcast.136, f32[768]{0:T(1024)S(1)} %copy-done.7, bf16[768,2304]{1,0:T(8,128)(2,1)} %constant_dynamic-update-slice_fusion, bf16[40,8,768]{2,1,0:T(8,128)(2,1)S(1)} %get-tuple-element.16, ...), kind=kOutput, calls=%fused_computation.69 | convolution fusion | flops 1137622784 | bytes 6983936 | tf_op jit(solution)/shard_map/dot_general | solution.py:84
  137.2 17.5 %all_to_all.84 = bf16[40,8,768]{2,1,0:T(8,128)(2,1)S(1)} all-to-all(bf16[40,8,768]{2,1,0:T(8,128)(2,1)S(1)} %add_convert_fusion.1), channel_id=1, replica_groups=mesh['tr'=4,'gz'=8] {'gz'}, dimensions={0} | all-to-all | bytes 983040 | tf_op jit(solution)/shard_map/all_to_all | solution.py:154
  155.3 1.4 fusion.79
  156.7 3.2 %fusion.49 = bf16[40,8,768]{2,1,0:T(8,128)(2,1)} fusion(f32[40,6,8,8]{2,3,1,0:T(8,128)S(1)} %fusion.79, bf16[40,8,2304]{2,1,0:T(8,128)(2,1)} %convolution_convert_fusion.1, f32[40,6,8,8]{2,3,1,0:T(8,128)} %copy-done.9, f32[40,6,8]{2,1,0:T(8,128)S(1)} %copy-done.11), kind=kOutput, calls=%fused_computation.56 | convolution fusion | flops 4287367 | bytes 4321280 | tf_op jit(solution)/shard_map/bhlm,bmhe->blhe/dot_general | solution.py:75
  159.9 3.1 %fusion.50 = bf16[40,8,768]{2,1,0:T(8,128)(2,1)} fusion(f32[40,6,8,8]{2,3,1,0:T(8,128)S(1)} %fusion.79, bf16[40,8,2304]{2,1,0:T(8,128)(2,1)} %convolution_convert_fusion.1, f32[40,6,8,8]{2,3,1,0:T(8,128)} %copy-done.9, f32[40,6,8]{2,1,0:T(8,128)S(1)} %copy-done.11), kind=kOutput, calls=%fused_computation.57 | convolution fusion | flops 4287367 | bytes 4321280 | tf_op jit(solution)/shard_map/bhlm,blhe->bmhe/dot_general | solution.py:78
  163.0 1.8 fusion.51
  165.3 2.6 %multiply_reduce_fusion.2 = (f32[40,8]{1,0:T(8,128)S(1)}, f32[40,8,768]{2,1,0:T(8,128)S(1)}) fusion(f32[40,8,768]{2,1,0:T(8,128)S(1)} %reshape.140, f32[768]{0:T(1024)S(1)} %copy-done.8, bf16[768,2304]{1,0:T(8,128)(2,1)S(1)} %copy-done.5, bf16[40,8,768]{2,1,0:T(8,128)(2,1)S(1)} %fusion.51, bf16[40,8,768]{2,1,0:T(8,128)(2,1)} %fusion.50, ...), kind=kOutput, calls=%fused_computation.67 | convolution fusion | flops 1137622784 | bytes 6983936 | tf_op jit(solution)/shard_map/dot_general | solution.py:84
  168.4 10.9 %all_to_all.85 = bf16[5,8,8,768]{3,1,0,2:T(8,128)(2,1)S(1)} all-to-all(bf16[5,8,8,768]{3,1,0,2:T(8,128)(2,1)S(1)} %copy.139), channel_id=1, replica_groups=mesh['tr'=4,'gz'=8] {'tr'}, dimensions={2} | all-to-all | bytes 983040 | tf_op jit(solution)/shard_map/all_to_all | solution.py:158
  (69 shorter events, 13.6 us)
Async XLA Ops:
  6.5 10.4 %copy-start.1 = (bf16[5,32,2,768]{3,2,1,0:T(2,128)(2,1)S(1)}, bf16[5,32,2,768]{3,2,1,0:T(2,128)(2,1)}, u32[]{:S(2)}) copy-start(bf16[5,32,2,768]{3,2,1,0:T(2,128)(2,1)} %param.9) | copy-start | bytes 1474564
  6.5 68.6 %all-gather.4.cloned.1.call-start = ((), (), s32[]{:S(2)}) async-start(), calls=%async_computation.6 | async-start | bytes 4423680 | tf_op jit(solution)/shard_map/all_gather | solution.py:107
  7.3 74.5 %all-gather.6.cloned.1.call-start = ((), (), s32[]{:S(2)}) async-start(), calls=%async_computation.7 | async-start | bytes 1474560 | tf_op jit(solution)/shard_map/all_gather | solution.py:108
  8.0 64.9 %collective-permute-start = (bf16[192,2304]{1,0:T(8,128)(2,1)}, bf16[192,2304]{1,0:T(8,128)(2,1)}, u32[]{:S(2)}, u32[]{:S(2)}) collective-permute-start(bf16[192,2304]{1,0:T(8,128)(2,1)} %param.14), channel_id=1, source_target_pairs={{0,8},{8,16},{16,24},{24,0},{1,9},{9,17},{17,25},{25,1},{2,10},{10... | collective-permute-start | bytes 2654216 | tf_op jit(solution)/shard_map/ppermute | solution.py:124
  8.5 88.2 %collective-permute-start.1 = (bf16[192,2304]{1,0:T(8,128)(2,1)}, bf16[192,2304]{1,0:T(8,128)(2,1)}, u32[]{:S(2)}, u32[]{:S(2)}) collective-permute-start(bf16[192,2304]{1,0:T(8,128)(2,1)} %param.14), channel_id=1, source_target_pairs={{0,24},{8,0},{16,8},{24,16},{1,25},{9,1},{17,9},{25,17},{2,26},{10... | collective-permute-start | bytes 2654216 | tf_op jit(solution)/shard_map/ppermute | solution.py:129
  12.7 40.3 %all-to-all-start.2 = ((bf16[5,32,2,768]{3,2,0,1:T(2,128)(2,1)}), bf16[5,32,2,768]{3,2,0,1:T(2,128)(2,1)S(1)}, u32[]{:S(2)}, u32[]{:S(2)}) async-start(bf16[5,32,2,768]{3,2,0,1:T(2,128)(2,1)} %copy.114), calls=%async_computation.2 | async-start | bytes 983040 | tf_op jit(solution)/shard_map/all_to_all | solution.py:142
  16.2 82.9 %all-gather.8.cloned.1.call-start = ((), (), s32[]{:S(2)}) async-start(), calls=%async_computation.8 | async-start | bytes 1474560 | tf_op jit(solution)/shard_map/all_gather | solution.py:139
  18.1 2.0 %copy-start = (bf16[192,2304]{1,0:T(8,128)(2,1)S(1)}, bf16[192,2304]{1,0:T(8,128)(2,1)}, u32[]{:S(2)}) copy-start(bf16[192,2304]{1,0:T(8,128)(2,1)} %param.14) | copy-start | bytes 2654212
  52.9 11.9 %all-to-all-start = ((bf16[5,32,2,768]{3,2,0,1:T(2,128)(2,1)}), bf16[5,32,2,768]{3,2,0,1:T(2,128)(2,1)S(1)}, u32[]{:S(2)}, u32[]{:S(2)}) async-start(bf16[5,32,2,768]{3,2,0,1:T(2,128)(2,1)} %copy.109), calls=%async_computation | async-start | bytes 983040 | tf_op jit(solution)/shard_map/all_to_all | solution.py:143
  65.9 9.3 %copy-start.8 = (f32[768]{0:T(1024)S(1)}, f32[768]{0:T(1024)}, u32[]{:S(2)}) copy-start(f32[768]{0:T(1024)} %param.10) | copy-start | bytes 9220
  65.9 27.1 %all-to-all-start.1 = ((bf16[5,64,768]{2,0,1:T(8,128)(2,1)}), bf16[5,64,768]{2,0,1:T(8,128)(2,1)S(1)}, u32[]{:S(2)}, u32[]{:S(2)}) async-start(bf16[5,64,768]{2,0,1:T(8,128)(2,1)} %bitcast.2), calls=%async_computation.1 | async-start | bytes 1572864 | tf_op jit(solution)/shard_map/all_to_all | solution.py:146
  73.0 28.7 %collective-permute-start.2 = (bf16[192,2304]{1,0:T(8,128)(2,1)}, bf16[192,2304]{1,0:T(8,128)(2,1)}, u32[]{:S(2)}, u32[]{:S(2)}) collective-permute-start(bf16[192,2304]{1,0:T(8,128)(2,1)} %collective-permute-done), channel_id=1, source_target_pairs={{0,8},{8,16},{16,24},{24,0},{1,9},{9,17},{17,25},{25,1},{2,10},{10... | collective-permute-start | bytes 2654216 | tf_op jit(solution)/shard_map/ppermute | solution.py:124
  81.7 2.8 %copy-start.9 = (f32[40,6,8,8]{2,3,1,0:T(8,128)}, f32[40,6,8,8]{2,3,1,0:T(8,128)S(1)}, u32[]{:S(2)}) copy-start(f32[40,6,8,8]{2,3,1,0:T(8,128)S(1)} %get-tuple-element.9) | copy-start | bytes 184324
  81.7 2.8 %copy-start.10 = (f32[40,6,8]{2,1,0:T(8,128)}, f32[40,6,8]{2,1,0:T(8,128)S(1)}, u32[]{:S(2)}) copy-start(f32[40,6,8]{2,1,0:T(8,128)S(1)} %get-tuple-element.8) | copy-start | bytes 23044
  93.0 23.9 %all-to-all-start.3 = ((bf16[5,64,768]{2,0,1:T(8,128)(2,1)}), bf16[5,64,768]{2,0,1:T(8,128)(2,1)S(1)}, u32[]{:S(2)}, u32[]{:S(2)}) async-start(bf16[5,64,768]{2,0,1:T(8,128)(2,1)} %copy.121), calls=%async_computation.3 | async-start | bytes 1572864 | tf_op jit(solution)/shard_map/all_to_all | solution.py:150
  103.9 13.6 %copy-start.7 = (f32[768]{0:T(1024)S(1)}, f32[768]{0:T(1024)}, u32[]{:S(2)}) copy-start(f32[768]{0:T(1024)} %param.13) | copy-start | bytes 9220
  120.8 1.1 copy-start.3
  131.2 1.8 copy-start.2
  131.2 2.0 %copy-start.4 = (bf16[40,8,6,128]{3,0,2,1:T(8,128)(2,1)S(1)}, bf16[40,8,6,128]{3,0,2,1:T(8,128)(2,1)}, u32[]{:S(2)}) copy-start(bf16[40,8,6,128]{3,0,2,1:T(8,128)(2,1)} %fusion.47) | copy-start | bytes 1474564
  137.1 17.5 %copy-start.6 = (bf16[768,768]{1,0:T(8,128)(2,1)S(1)}, bf16[768,768]{1,0:T(8,128)(2,1)}, u32[]{:S(2)}) copy-start(bf16[768,768]{1,0:T(8,128)(2,1)} %all-gather.6.cloned.1.call-done) | copy-start | bytes 3538948
  154.7 2.0 %copy-start.11 = (f32[40,6,8]{2,1,0:T(8,128)S(1)}, f32[40,6,8]{2,1,0:T(8,128)}, u32[]{:S(2)}) copy-start(f32[40,6,8]{2,1,0:T(8,128)} %copy-done.10) | copy-start | bytes 23044
  163.0 2.3 %copy-start.5 = (bf16[768,2304]{1,0:T(8,128)(2,1)S(1)}, bf16[768,2304]{1,0:T(8,128)(2,1)}, u32[]{:S(2)}) copy-start(bf16[768,2304]{1,0:T(8,128)(2,1)} %all-gather.4.cloned.1.call-done) | copy-start | bytes 10616836
Sparse Core Ops, SparseCore 0:
  8.9 47.7 all-gather.3
  58.2 19.5 all-gather.5
  79.4 17.3 all-gather.7
